TPU v7x, 512 devices: a whole 4x8x8 slice. The times are simulated.
512 devices in a mesh: req: 64 (over z, x, core), tp: 8 (over y).
Axes of the slice: x: 4, y: 8, z: 8, core: 2. Of those that a mesh axis runs over, the one named last changes fastest.
Arguments:
- normed_hidden_input: bfloat16 [1024, 2, 8192], P('req', None, 'tp'), may hold values from -6 to 6
- value_matrix: bfloat16 [8192, 1024], P(None, 'tp'), may hold values from -0.0625 to 0.0625
- adapter_down_weight: bfloat16 [8192, 32768], P('tp', 'req'), may hold values from -0.0625 to 0.0625
- adapter_up_weight: bfloat16 [32768, 1024], P('req', 'tp'), may hold values from -0.75 to 0.75
- request_adapter: int32 [1024], P('req'), may hold values from 0 to 511, as said below
- adapter_storage_row: int32 [512], replicated, may hold values from 0 to 511, as said below
- cache_valid_length: int32 [1024], P('req'), may hold values from 2 to 64
- queries: bfloat16 [1024, 2, 8192], P('req', None, 'tp'), may hold values from -9 to 9
- stored_key_cache: bfloat16 [1024, 64, 1024], P('req', None, 'tp'), may hold values from -4 to 4
- stored_value_cache: bfloat16 [1024, 64, 1024], P('req', None, 'tp'), may hold values from -6 to 6
- step_keys: bfloat16 [1024, 2, 1024], P('req', None, 'tp'), may hold values from -6 to 6
Outputs:
- step_values: bfloat16 [1024, 2, 1024], P('req', None, 'tp')
- attention: bfloat16 [1024, 2, 8192], P('req', None, 'tp')
Inputs may be any that keep to these rules, and one draw needn't show every extreme that they name: `request_adapter`: storage row p lies on home device p // 8. Of the 16 requests of one device, at most 2 use adapters stored on one home device; one home device gets exactly 2 from every device. `adapter_storage_row`: A permutation.
All inputs are finite; a program needn't handle non-finite values.
Results may differ from a plain program's by a relative error of at most 0.0053.
Values may be sent and summed in bfloat16 or wider, within the bound.
No kernel may reach another device: no remote copies, remote signals or barrier semaphores. Data moves between devices by JAX's collectives and lax.ppermute only.
A program may use at most 64 MiB of HBM per device.

v0:
```python
import math
import jax
import jax.numpy as jnp
from jax import lax
from jax.sharding import PartitionSpec as P

HEAD_WIDTH = 128
ADAPTER_RANK = 64
QUERY_PER_KEY = 8


def body(
    normed_hidden_input,
    value_matrix,
    adapter_down_weight,
    adapter_up_weight,
    request_adapter,
    adapter_storage_row,
    cache_valid_length,
    queries,
    stored_key_cache,
    stored_value_cache,
    step_keys,
):
    req_local, step_count, width_local = normed_hidden_input.shape
    value_local = value_matrix.shape[1]
    adapter_delta = adapter_up_weight.shape[0] // ADAPTER_RANK
    my_index = lax.axis_index("req")
    total_adapters = adapter_storage_row.shape[0]
    matches = request_adapter[:, None] == jnp.arange(total_adapters, dtype=jnp.int32)[None, :]
    storage = jnp.sum(jnp.where(matches, adapter_storage_row[None, :], 0), axis=1)
    columns_in = lax.all_gather(normed_hidden_input, "tp", axis=2, tiled=True)
    span = columns_in.shape[2]
    product = jnp.dot(
        columns_in.reshape(-1, span), value_matrix, preferred_element_type=jnp.float32
    )
    plain_values = product.reshape(
        jnp.zeros((req_local, step_count, value_local), jnp.float32).shape
    )
    every_row, every_storage = (
        lax.all_gather(normed_hidden_input, "req", axis=0, tiled=True),
        lax.all_gather(storage, "req", axis=0, tiled=True),
    )
    every_slot = jnp.where(
        every_storage // adapter_delta == my_index, every_storage % adapter_delta, -1
    )
    row_count = every_row.shape[0]
    projected = jnp.dot(
        every_row.reshape(row_count * step_count, width_local),
        adapter_down_weight,
        preferred_element_type=jnp.float32,
    )
    projected = projected.reshape(row_count, step_count, adapter_delta, ADAPTER_RANK)
    chosen = (every_slot[:, None] == jnp.arange(adapter_delta, dtype=jnp.int32)[None, :]).astype(
        jnp.float32
    )
    partial_value = jnp.einsum("nsar,na->nsr", projected, chosen)
    summed_all = lax.psum(partial_value, "tp").astype(jnp.bfloat16)
    row_count = summed_all.shape[0]
    chosen = (
        every_slot[:, None, None, None]
        == jnp.arange(adapter_delta, dtype=jnp.int32)[None, None, :, None]
    )
    spread = jnp.where(chosen, summed_all[:, :, None, :], jnp.zeros((), jnp.bfloat16))
    product = jnp.dot(
        spread.reshape(row_count * step_count, adapter_delta * ADAPTER_RANK),
        adapter_up_weight,
        preferred_element_type=jnp.float32,
    )
    low_rank = lax.psum_scatter(
        product.reshape(row_count, step_count, value_local), "req", scatter_dimension=0, tiled=True
    ).astype(jnp.bfloat16)
    low_rank = lax.optimization_barrier(low_rank)
    step_values = (plain_values + low_rank.astype(jnp.float32)).astype(jnp.bfloat16)
    kv_local = value_local // HEAD_WIDTH
    scale = 1.0 / math.sqrt(HEAD_WIDTH)
    query_head_view = queries.reshape(req_local, step_count, kv_local, QUERY_PER_KEY, HEAD_WIDTH)
    key_head_view = stored_key_cache.reshape(req_local, -1, kv_local, HEAD_WIDTH)
    value_view = stored_value_cache.reshape(req_local, -1, kv_local, HEAD_WIDTH)
    current_keys = step_keys.reshape(req_local, step_count, kv_local, HEAD_WIDTH)
    fresh_values = step_values.reshape(req_local, step_count, kv_local, HEAD_WIDTH)
    context = key_head_view.shape[1]
    cache_scores = (
        jnp.einsum(
            "rskgd,rckd->rskgc", query_head_view, key_head_view, preferred_element_type=jnp.float32
        )
        * scale
    )
    fresh_scores = (
        jnp.einsum(
            "rskgd,rtkd->rskgt", query_head_view, current_keys, preferred_element_type=jnp.float32
        )
        * scale
    )
    valid = jnp.arange(context, dtype=jnp.int32)[None, :] < cache_valid_length[:, None]
    causal = (
        jnp.arange(step_count, dtype=jnp.int32)[None, :]
        <= jnp.arange(step_count, dtype=jnp.int32)[:, None]
    )
    cache_scores = jnp.where(valid[:, None, None, None, :], cache_scores, -jnp.inf)
    fresh_scores = jnp.where(causal[None, :, None, None, :], fresh_scores, -jnp.inf)
    peak = jnp.maximum(jnp.max(cache_scores, axis=-1), jnp.max(fresh_scores, axis=-1))[..., None]
    cache_expo = jnp.exp(cache_scores - peak)
    fresh_expo = jnp.exp(fresh_scores - peak)
    denominator = jnp.sum(cache_expo, axis=-1, keepdims=True) + jnp.sum(
        fresh_expo, axis=-1, keepdims=True
    )
    cache_weights = (cache_expo / denominator).astype(jnp.bfloat16)
    fresh_weights = (fresh_expo / denominator).astype(jnp.bfloat16)
    attended = jnp.einsum(
        "rskgc,rckd->rskgd", cache_weights, value_view, preferred_element_type=jnp.float32
    )
    attended = attended + jnp.einsum(
        "rskgt,rtkd->rskgd", fresh_weights, fresh_values, preferred_element_type=jnp.float32
    )
    attention = attended.astype(jnp.bfloat16).reshape(
        req_local, step_count, kv_local * QUERY_PER_KEY * HEAD_WIDTH
    )
    return (step_values, attention)


def solution(mesh):
    placed = (
        P("req", None, "tp"),
        P(None, "tp"),
        P("tp", "req"),
        P("req", "tp"),
        P("req"),
        P(),
        P("req"),
        P("req", None, "tp"),
        P("req", None, "tp"),
        P("req", None, "tp"),
        P("req", None, "tp"),
    )
    return jax.shard_map(
        body,
        mesh=mesh,
        in_specs=placed,
        out_specs=(P("req", None, "tp"), P("req", None, "tp")),
        check_vma=False,
    )
```

profile of v0, /device:TPU:8, one launch (start us, length us, event | category | flops | bytes accessed | tf_op | source)
XLA Modules:
  0.0 298.1 jit_solution(1287845142571132430)
XLA Ops:
  7.2 0.7 all-gather.2.cloned.1.call-update
  8.0 1.5 copy.28
  9.5 1.3 dynamic-slice
  11.4 0.2 select_reduce_fusion
  11.6 0.2 dynamic-update-slice
  11.9 26.9 %all-reduce = s32[1024]{0:T(1024)S(1)} all-reduce(s32[1024]{0:T(1024)S(1)} %dynamic-update-slice), channel_id=1, replica_groups=mesh['req'=64,'tp'=8] {'req'}, use_global_device_ids=true, to_apply=%add | all-reduce | flops 1024 | bytes 8192
  38.8 62.3 %all-gather.2.cloned.1.call-done = bf16[1024,2,1024]{2,1,0:T(2,128)(2,1)} async-done(((bf16[16,2,1024]{2,1,0:T(2,128)(2,1)}), bf16[1024,2,1024]{2,1,0:T(2,128)(2,1)}) %all-gather.2.cloned.1.call-update) | async-done | bytes 4194320 | tf_op jit(solution)/shard_map/all_gather | solution.py:41
  101.1 5.5 %multiply_reduce_fusion = f32[1024,2,64]{0,2,1:T(8,128)} fusion(bf16[8,64,1024,1]{2,1,0,3:T(8,128)(2,1)S(1)} %bitcast.84, bf16[1024,2,1024,1]{2,1,0,3:T(2,128)(2,1)} %bitcast.86, f32[1024,8]{0,1:T(8,128)S(1)} %get-tuple-element.10), kind=kOutput, calls=%fused_computation.2 | convolution fusion | flops 2149449728 | bytes 5799936 | tf_op jit(solution)/shard_map/dot_general | solution.py:48
  106.6 35.4 %all-reduce.2 = bf16[1024,2,64]{0,2,1:T(8,128)(2,1)S(1)} all-reduce(f32[1024,2,64]{0,2,1:T(8,128)} %multiply_reduce_fusion), channel_id=1, replica_groups=mesh['req'=64,'tp'=8] {'tp'}, use_global_device_ids=true, to_apply=%region_1.2 | all-reduce | flops 131072 | bytes 786432 | tf_op jit(solution)/shard_map/psum | solution.py:58
  142.0 0.1 broadcast_in_dim.83
  142.2 0.3 bitcast_select_fusion
  142.6 1.7 fusion.22
  144.5 0.4 fusion.39
  145.0 0.3 fusion.38
  145.3 0.1 fusion.27
  145.4 0.2 fusion.24
  145.6 25.3 %all_gather.9 = bf16[16,2,8192]{2,0,1:T(8,128)(2,1)S(1)} all-gather(bf16[16,2,1024]{2,0,1:T(8,128)(2,1)S(1)} %copy.27), channel_id=1, replica_groups=mesh['req'=64,'tp'=8] {'tp'}, dimensions={2}, use_global_device_ids=true | all-gather | bytes 589824 | tf_op jit(solution)/shard_map/all_gather | solution.py:32
  171.0 117.4 %reduce-scatter.2.cloned.1.call-done = f32[16,2,128]{2,0,1:T(8,128)} async-done(((f32[1024,2,128]{2,0,1:T(8,128)}), f32[16,2,128]{2,0,1:T(8,128)}) %reduce-scatter.2.cloned.1.call-update) | async-done | bytes 16400 | tf_op jit(solution)/shard_map/reduce_scatter | solution.py:70
  288.4 0.7 convert_element_type.29
  289.1 0.4 fusion.16
  289.5 0.6 copy.32
  290.1 0.2 fusion.28
  290.4 0.3 fusion.11
  290.6 0.7 reshape.157
  (32 shorter events, 0.4 us)
Async XLA Ops:
  7.2 281.9 %copy-start = (bf16[8192,128]{1,0:T(8,128)(2,1)S(1)}, bf16[8192,128]{1,0:T(8,128)(2,1)}, u32[]{:S(2)}) copy-start(bf16[8192,128]{1,0:T(8,128)(2,1)} %param.12) | copy-start | bytes 6291460
  7.2 4.2 %copy-start.7 = (s32[16]{0:T(128)S(1)}, s32[16]{0:T(128)}, u32[]{:S(2)}) copy-start(s32[16]{0:T(128)} %param.15) | copy-start | bytes 196
  7.2 4.2 %copy-start.5 = (s32[512]{0:T(512)S(1)}, s32[512]{0:T(512)}, u32[]{:S(2)}) copy-start(s32[512]{0:T(512)} %param.16) | copy-start | bytes 6148
  7.2 93.9 %all-gather.2.cloned.1.call-start = ((), (), s32[]{:S(2)}) async-start(), calls=%async_computation.1 | async-start | bytes 4259840 | tf_op jit(solution)/shard_map/all_gather | solution.py:41
  7.9 280.4 %reduce-scatter.2.cloned.1.call-start = ((), (), s32[]{:S(2)}) async-start(), calls=%async_computation.2 | async-start | bytes 1064960 | tf_op jit(solution)/shard_map/reduce_scatter | solution.py:70
  106.6 35.9 %copy-start.3 = (bf16[512,128]{1,0:T(8,128)(2,1)S(1)}, bf16[512,128]{1,0:T(8,128)(2,1)}, u32[]{:S(2)}) copy-start(bf16[512,128]{1,0:T(8,128)(2,1)} %param.14) | copy-start | bytes 393220
  142.5 1.8 copy-start.2
  142.5 1.9 copy-start.4
  142.5 1.9 copy-start.6
  142.5 2.0 copy-start.9
  142.6 2.4 copy-start.1
  145.3 145.1 %copy-start.8 = (bf16[16,64,128]{2,1,0:T(8,128)(2,1)S(1)}, bf16[16,64,128]{2,1,0:T(8,128)(2,1)}, u32[]{:S(2)}) copy-start(bf16[16,64,128]{2,1,0:T(8,128)(2,1)} %param.20) | copy-start | bytes 786436
Sparse Core Ops, SparseCore 0:
  11.4 89.6 all-gather.1
  144.5 143.8 reduce-scatter.1
where the time goes:
time: 298 us
  waiting for transfers between devices  180 us (60%)
  blocking collectives  87.7 us (29%)
  between operations  14.9 us (5%)
  matrix products  8.95 us (3%)
  local copies, waits for them, and re-layouts  4.54 us (2%)
    reduce_scatter x1, waiting for transfers between devices, body(): lax.psum_scatter(product.reshape(row_count, step_count, value_local), 're...  117 us
    all_gather x1, waiting for transfers between devices, body(): lax.all_gather(normed_hidden_input, 'req', axis=0, tiled=True)  62.3 us
    psum x1, blocking collectives, body(): summed_all = lax.psum(partial_value, 'tp').astype(jnp.bfloat16)  35.4 us
    unnamed x1, blocking collectives  26.9 us
    all_gather x1, blocking collectives, body(): columns_in = lax.all_gather(normed_hidden_input, 'tp', axis=2, tiled=True)  25.3 us
  transfers between devices with their start and end apart: 2, of which 2 were waited for; matrix products, arithmetic and copies ran while one was open for 1% of the time, Pallas kernels for 0%

commit v1 on v0

--- a/solution.py
+++ b/solution.py
@@ -55,7 +55,7 @@
         jnp.float32
     )
     partial_value = jnp.einsum("nsar,na->nsr", projected, chosen)
-    summed_all = lax.psum(partial_value, "tp").astype(jnp.bfloat16)
+    summed_all = jnp.sum(lax.all_gather(partial_value, "tp"), axis=0).astype(jnp.bfloat16)
     row_count = summed_all.shape[0]
     chosen = (
         every_slot[:, None, None, None]

time: 298 us -> 332 us (1.11)
  waiting for transfers between devices: 180 us -> 237 us
  blocking collectives: 87.7 us -> 53.5 us
  local copies, waits for them, and re-layouts: 4.54 us -> 12.7 us
    all_gather x0 -> x1, waiting for transfers between devices: none -> 52.7 us  [body(): lax.all_gather(partial_value, 'tp')]
    psum x1 -> x0, blocking collectives: 35.4 us -> none  [body(): summed_all = lax.psum(partial_value, 'tp').astype(jnp.bfloat16)]
    unnamed x26 -> x27, local copies, waits for them, and re-layouts: 3.69 us -> 11.8 us
    reduce_scatter x1, waiting for transfers between devices: 117 us -> 121 us  [body(): lax.psum_scatter(product.reshape(row_count, step_count, value_local), 're...]
  transfers between devices with their start and end apart: 2 -> 3, of which waited for: 2 -> 3; matrix products, arithmetic and copies ran while one was open for 1% -> 1% of each run, Pallas kernels for 0% -> 0%
where the time goes in v1:
time: 332 us; the launch traced here: 331 us
  waiting for transfers between devices  237 us (71%)
  blocking collectives  53.5 us (16%)
  between operations  14.6 us (4%)
  local copies, waits for them, and re-layouts  12.7 us (4%)
  matrix products  8.95 us (3%)
  other arithmetic  4.84 us (1%)
    reduce_scatter x1, waiting for transfers between devices, body(): lax.psum_scatter(product.reshape(row_count, step_count, value_local), 're...  121 us
    all_gather x1, waiting for transfers between devices, body(): lax.all_gather(normed_hidden_input, 'req', axis=0, tiled=True)  62.3 us
    all_gather x1, waiting for transfers between devices, body(): lax.all_gather(partial_value, 'tp')  52.7 us
    unnamed x1, blocking collectives  26.9 us
    all_gather x1, blocking collectives, body(): columns_in = lax.all_gather(normed_hidden_input, 'tp', axis=2, tiled=True)  26.5 us
    unnamed x27, local copies, waits for them, and re-layouts  11.8 us
  transfers between devices with their start and end apart: 3, of which 3 were waited for; matrix products, arithmetic and copies ran while one was open for 1% of the time, Pallas kernels for 0%

profile of v1, /device:TPU:8, one launch (start us, length us, event | category | flops | bytes accessed | tf_op | source)
XLA Modules:
  0.0 331.4 jit_solution(10626191122772089524)
XLA Ops:
  7.2 0.7 all-gather.4.cloned.1.call-update
  8.0 1.5 copy.28
  9.5 1.3 dynamic-slice
  11.6 0.2 dynamic-update-slice
  11.9 26.9 %all-reduce = s32[1024]{0:T(1024)S(1)} all-reduce(s32[1024]{0:T(1024)S(1)} %dynamic-update-slice), channel_id=1, replica_groups=mesh['req'=64,'tp'=8] {'req'}, use_global_device_ids=true, to_apply=%add | all-reduce | flops 1024 | bytes 8192
  38.8 62.3 %all-gather.4.cloned.1.call-done = bf16[1024,2,1024]{2,1,0:T(2,128)(2,1)} async-done(((bf16[16,2,1024]{2,1,0:T(2,128)(2,1)}), bf16[1024,2,1024]{2,1,0:T(2,128)(2,1)}) %all-gather.4.cloned.1.call-update) | async-done | bytes 4194320 | tf_op jit(solution)/shard_map/all_gather | solution.py:41
  101.1 5.5 %multiply_reduce_fusion = f32[1024,2,64]{0,2,1:T(8,128)} fusion(bf16[8,64,1024,1]{2,1,0,3:T(8,128)(2,1)S(1)} %bitcast.92, bf16[1024,2,1024,1]{2,1,0,3:T(2,128)(2,1)} %bitcast.94, f32[1024,8]{0,1:T(8,128)S(1)} %get-tuple-element.10), kind=kOutput, calls=%fused_computation.2 | convolution fusion | flops 2149449728 | bytes 5799936 | tf_op jit(solution)/shard_map/dot_general | solution.py:48
  106.7 52.7 %all-gather.6.cloned.1.call-done = f32[8192,2,64]{0,2,1:T(8,128)} async-done(((f32[1024,2,64]{0,2,1:T(8,128)}), f32[8192,2,64]{0,2,1:T(8,128)}) %all-gather.6.cloned.1.call-update) | async-done | bytes 4194320 | tf_op jit(solution)/shard_map/all_gather | solution.py:58
  159.4 7.7 %copy.49 = f32[16,8,8,1024]{3,2,1,0:T(8,128)} copy(f32[16,8,8,1024]{3,1,2,0:T(8,128)} %bitcast.90) | data formatting | bytes 8388608
  167.1 3.2 reduce_sum.37
  170.5 0.3 bitcast_select_fusion
  170.8 0.4 copy-done.3
  171.3 1.7 fusion.22
  173.2 0.4 fusion.39
  173.7 0.3 fusion.38
  174.1 0.2 fusion.24
  174.3 26.5 %all_gather.15 = bf16[16,2,8192]{2,0,1:T(8,128)(2,1)S(1)} all-gather(bf16[16,2,1024]{2,0,1:T(8,128)(2,1)S(1)} %copy.27), channel_id=1, replica_groups=mesh['req'=64,'tp'=8] {'tp'}, dimensions={2}, use_global_device_ids=true | all-gather | bytes 589824 | tf_op jit(solution)/shard_map/all_gather | solution.py:32
  200.9 121.1 %reduce-scatter.2.cloned.1.call-done = f32[16,2,128]{2,0,1:T(8,128)} async-done(((f32[1024,2,128]{2,0,1:T(8,128)}), f32[16,2,128]{2,0,1:T(8,128)}) %reduce-scatter.2.cloned.1.call-update) | async-done | bytes 16400 | tf_op jit(solution)/shard_map/reduce_scatter | solution.py:70
  321.9 0.7 convert_element_type.33
  322.7 0.4 fusion.16
  323.1 0.6 copy.32
  323.7 0.2 fusion.28
  323.9 0.3 fusion.11
  324.2 0.7 reshape.159
  (36 shorter events, 0.8 us)
Async XLA Ops:
  7.2 315.5 %copy-start = (bf16[8192,128]{1,0:T(8,128)(2,1)S(1)}, bf16[8192,128]{1,0:T(8,128)(2,1)}, u32[]{:S(2)}) copy-start(bf16[8192,128]{1,0:T(8,128)(2,1)} %param.12) | copy-start | bytes 6291460
  7.2 4.2 %copy-start.7 = (s32[16]{0:T(128)S(1)}, s32[16]{0:T(128)}, u32[]{:S(2)}) copy-start(s32[16]{0:T(128)} %param.15) | copy-start | bytes 196
  7.2 4.2 %copy-start.5 = (s32[512]{0:T(512)S(1)}, s32[512]{0:T(512)}, u32[]{:S(2)}) copy-start(s32[512]{0:T(512)} %param.16) | copy-start | bytes 6148
  7.2 93.9 %all-gather.4.cloned.1.call-start = ((), (), s32[]{:S(2)}) async-start(), calls=%async_computation.1 | async-start | bytes 4259840 | tf_op jit(solution)/shard_map/all_gather | solution.py:41
  7.9 151.5 %all-gather.6.cloned.1.call-start = ((), (), s32[]{:S(2)}) async-start(), calls=%async_computation.3 | async-start | bytes 4718592 | tf_op jit(solution)/shard_map/all_gather | solution.py:58
  106.6 215.3 %reduce-scatter.2.cloned.1.call-start = ((), (), s32[]{:S(2)}) async-start(), calls=%async_computation.2 | async-start | bytes 1064960 | tf_op jit(solution)/shard_map/reduce_scatter | solution.py:70
  170.3 0.9 copy-start.3
  171.3 1.8 copy-start.2
  171.3 1.8 copy-start.4
  171.3 1.9 copy-start.6
  171.3 2.0 copy-start.9
  171.3 2.4 copy-start.1
  174.0 149.9 %copy-start.8 = (bf16[16,64,128]{2,1,0:T(8,128)(2,1)S(1)}, bf16[16,64,128]{2,1,0:T(8,128)(2,1)}, u32[]{:S(2)}) copy-start(bf16[16,64,128]{2,1,0:T(8,128)(2,1)} %param.20) | copy-start | bytes 786436
Sparse Core Ops, SparseCore 0:
  11.4 89.6 all-gather.3
  106.8 52.5 all-gather.5
  173.2 148.7 reduce-scatter.1
